TPU v7x, 32 devices: a whole 2x2x4 slice. The times are simulated.
32 devices in a mesh: drive: 2 (over y), tm: 4 (over z), mom: 2 (over x), col: 2 (over core).
Axes of the slice: x: 2, y: 2, z: 4, core: 2. Of those that a mesh axis runs over, the one named last changes fastest.
Arguments:
- propagators: float32 [8, 8, 384, 384], P(('drive', 'mom'), 'tm', None, 'col'), parts along dimension 0, as said below
- current_op: float32 [4, 384, 384], P('mom'), may hold values from -6 to 6
Outputs:
- spectrum: float32 [8, 2, 8, 384, 384], P(('drive', 'mom'), None, None, 'tm', 'col'), parts along dimension 0
There are 2 independent parts, one for each index of `drive`. A program takes and returns all parts, laid end to end along the dimension named above; an argument that names none is the same for every part. Nothing has to cross between parts.
Inputs may be any that keep to these rules, and one draw needn't show every extreme that they name: Every matrix propagators[k, t] is orthogonal to float32 rounding, with dense entries.
All inputs are finite; a program needn't handle non-finite values.
Results may differ from a plain program's by a relative error of at most 0.0003.
Values sent between devices are 32-bit elements; how exact they have to be, the bound alone decides.
A program may use at most 64 MiB of HBM per device.

v0:
```python
import math

import jax
import jax.numpy as jnp
from jax import lax
from jax.sharding import PartitionSpec as P


def prefix_2(value, axis, join, neutral):
    count, mine = (lax.axis_size(axis), lax.axis_index(axis))
    pieces = lax.all_gather(value, axis)
    running = jnp.full_like(value, 0) + jnp.asarray(neutral, value.dtype)

    def turn(position, running):
        longer = join(running, pieces[position])
        return jnp.where(position < mine, longer, running)

    return lax.fori_loop(0, count - 1, turn, running)


def multiply(left, right):
    return jnp.einsum("kab,kbc->kac", left, right, precision=lax.Precision.HIGHEST)


def later_first(earlier, later):
    return multiply(later, earlier)


def chain_step(carry, unit):
    nxt = multiply(unit, carry)
    return (nxt, nxt)


def spectrum_block(block):
    length = block.shape[1]
    freq = lax.broadcasted_iota(jnp.int32, (length, length), 0)
    times = lax.broadcasted_iota(jnp.int32, (length, length), 1)
    phase = 2.0 * math.pi / length * (freq * times % length).astype(jnp.float32)
    scale = 1.0 / math.sqrt(length)
    cosine = jnp.cos(phase) * scale
    sine = -jnp.sin(phase) * scale
    real = jnp.einsum("ft,ktrc->kfrc", cosine, block, precision=lax.Precision.HIGHEST)
    imag = jnp.einsum("ft,ktrc->kfrc", sine, block, precision=lax.Precision.HIGHEST)
    return jnp.stack([real, imag], axis=1)


def owner_block(block):
    return spectrum_block(block[:, :, 0])


def body(propagators, current_op):
    sym = 0.5 * (current_op + jnp.swapaxes(current_op, 1, 2))
    whole = lax.all_to_all(propagators, "col", split_axis=1, concat_axis=3, tiled=True)
    kdev = whole.shape[0]
    order = whole.shape[2]
    units = jnp.moveaxis(whole, 1, 0)
    total = units[0]
    identity = jnp.broadcast_to(jnp.eye(order, dtype=jnp.float32), total.shape)
    carry_in = prefix_2(total, ("tm", "col"), later_first, identity)
    _, applied = lax.scan(chain_step, carry_in, units)
    prefix = jnp.moveaxis(applied, 0, 1)
    weighted = jnp.einsum("kab,ksbc->ksac", sym, prefix, precision=lax.Precision.HIGHEST)
    n_rows = lax.axis_size("tm")
    n_cols = lax.axis_size("col")
    row_width = order // n_rows
    col_width = order // n_cols
    slices = prefix.shape[1]
    left = prefix.reshape(kdev, slices, order, n_rows, row_width)
    right = weighted.reshape(kdev, slices, order, n_cols, col_width)
    heis = jnp.einsum("ksbir,ksbjq->ksijrq", left, right, precision=lax.Precision.HIGHEST)
    heis = heis.reshape(kdev, slices, n_rows * n_cols, row_width, col_width)
    return owner_block(lax.all_to_all(heis, ("tm", "col"), split_axis=2, concat_axis=1, tiled=True))


def solution(mesh):
    return jax.shard_map(
        body,
        mesh=mesh,
        in_specs=(P(("drive", "mom"), "tm", None, "col"), P("mom", None, None)),
        out_specs=P(("drive", "mom"), None, None, "tm", "col"),
        check_vma=False,
    )
```

profile of v0, /device:TPU:0, one launch (start us, length us, event | category | flops | bytes accessed | tf_op | source)
XLA Modules:
  0.0 198.6 jit_solution(8359196111122669494)
XLA Ops:
  6.5 0.0 all-gather.2.cloned.1.call-start
  6.5 1.3 copy.15
  7.9 4.7 %all_to_all.24 = f32[2,2,384,192]{2,3,0,1:T(8,128)S(1)} all-to-all(f32[2,2,384,192]{2,3,0,1:T(8,128)S(1)} %copy.15), channel_id=1, replica_groups=mesh['drive'=2,'tm'=4,'mom'=2,'col'=2] {'col'}, dimensions={1} | all-to-all | bytes 2359296 | tf_op jit(solution)/shard_map/all_to_all | solution.py:53
  12.6 0.1 copy.16
  12.7 1.4 copy.17
  14.0 0.0 copy-start
  14.0 0.0 all-gather.2.cloned.1.call-update
  14.1 1.2 copy-done
  15.3 1.4 copy.20
  16.7 0.9 fusion.19
  17.5 90.1 %all-gather.2.cloned.1.call-done = f32[8,2,384,384]{3,2,1,0:T(8,128)} async-done(((f32[1,2,384,384]{3,2,1,0:T(8,128)}), f32[8,2,384,384]{3,2,1,0:T(8,128)}) %all-gather.2.cloned.1.call-update) | async-done | bytes 9437200 | tf_op jit(solution)/shard_map/all_gather | solution.py:11
  107.7 1.1 broadcast_in_dim.7
  108.8 26.5 %while.8 = (s32[]{:T(128)}, f32[2,384,384]{2,1,0:T(8,128)S(1)}, s32[]{:T(128)}, f32[8,2,384,384]{3,2,1,0:T(8,128)}, s32[]{:T(128)}) while((s32[]{:T(128)}, f32[2,384,384]{2,1,0:T(8,128)S(1)}, s32[]{:T(128)}, f32[8,2,384,384]{3,2,1,0:T(8,128)}, s32[]{:T(128)}) %tuple.31), condition=%wide.region_1.2_spmd, body=%wide.region_0.1_spmd.sunk | while | flops 1359249408 | bytes 7077971 | solution.py:18
  108.8 0.1 copy.48
  108.9 3.7 %convolution_select_fusion.2 = f32[2,384,384]{2,1,0:T(8,128)S(1)} fusion(f32[2,384,384]{2,1,0:T(8,128)S(1)} %copy.48, f32[8,2,384,384]{3,2,1,0:T(8,128)} %get-tuple-element.147, s32[]{:T(128)S(6)} %copy.41, pred[]{:T(512)S(6)} %lt.40), kind=kOutput, calls=%fused_computation.clone.1 | convolution fusion | flops 1359249408 | bytes 4718597 | tf_op jit(solution)/shard_map/while/body/eval_jaxpr/kab,kbc->kac/dot_general | solution.py:22
  112.6 0.1 copy.48
  112.7 3.7 %convolution_select_fusion.2 = f32[2,384,384]{2,1,0:T(8,128)S(1)} fusion(f32[2,384,384]{2,1,0:T(8,128)S(1)} %copy.48, f32[8,2,384,384]{3,2,1,0:T(8,128)} %get-tuple-element.147, s32[]{:T(128)S(6)} %copy.41, pred[]{:T(512)S(6)} %lt.40), kind=kOutput, calls=%fused_computation.clone.1 | convolution fusion | flops 1359249408 | bytes 4718597 | tf_op jit(solution)/shard_map/while/body/eval_jaxpr/kab,kbc->kac/dot_general | solution.py:22
  116.4 0.1 copy.48
  116.5 3.7 %convolution_select_fusion.2 = f32[2,384,384]{2,1,0:T(8,128)S(1)} fusion(f32[2,384,384]{2,1,0:T(8,128)S(1)} %copy.48, f32[8,2,384,384]{3,2,1,0:T(8,128)} %get-tuple-element.147, s32[]{:T(128)S(6)} %copy.41, pred[]{:T(512)S(6)} %lt.40), kind=kOutput, calls=%fused_computation.clone.1 | convolution fusion | flops 1359249408 | bytes 4718597 | tf_op jit(solution)/shard_map/while/body/eval_jaxpr/kab,kbc->kac/dot_general | solution.py:22
  120.2 0.1 copy.48
  120.3 3.7 %convolution_select_fusion.2 = f32[2,384,384]{2,1,0:T(8,128)S(1)} fusion(f32[2,384,384]{2,1,0:T(8,128)S(1)} %copy.48, f32[8,2,384,384]{3,2,1,0:T(8,128)} %get-tuple-element.147, s32[]{:T(128)S(6)} %copy.41, pred[]{:T(512)S(6)} %lt.40), kind=kOutput, calls=%fused_computation.clone.1 | convolution fusion | flops 1359249408 | bytes 4718597 | tf_op jit(solution)/shard_map/while/body/eval_jaxpr/kab,kbc->kac/dot_general | solution.py:22
  124.0 0.1 copy.48
  124.1 3.7 %convolution_select_fusion.2 = f32[2,384,384]{2,1,0:T(8,128)S(1)} fusion(f32[2,384,384]{2,1,0:T(8,128)S(1)} %copy.48, f32[8,2,384,384]{3,2,1,0:T(8,128)} %get-tuple-element.147, s32[]{:T(128)S(6)} %copy.41, pred[]{:T(512)S(6)} %lt.40), kind=kOutput, calls=%fused_computation.clone.1 | convolution fusion | flops 1359249408 | bytes 4718597 | tf_op jit(solution)/shard_map/while/body/eval_jaxpr/kab,kbc->kac/dot_general | solution.py:22
  127.8 0.1 copy.48
  127.8 3.7 %convolution_select_fusion.2 = f32[2,384,384]{2,1,0:T(8,128)S(1)} fusion(f32[2,384,384]{2,1,0:T(8,128)S(1)} %copy.48, f32[8,2,384,384]{3,2,1,0:T(8,128)} %get-tuple-element.147, s32[]{:T(128)S(6)} %copy.41, pred[]{:T(512)S(6)} %lt.40), kind=kOutput, calls=%fused_computation.clone.1 | convolution fusion | flops 1359249408 | bytes 4718597 | tf_op jit(solution)/shard_map/while/body/eval_jaxpr/kab,kbc->kac/dot_general | solution.py:22
  131.5 0.1 copy.48
  131.6 3.7 %convolution_select_fusion.2 = f32[2,384,384]{2,1,0:T(8,128)S(1)} fusion(f32[2,384,384]{2,1,0:T(8,128)S(1)} %copy.48, f32[8,2,384,384]{3,2,1,0:T(8,128)} %get-tuple-element.147, s32[]{:T(128)S(6)} %copy.41, pred[]{:T(512)S(6)} %lt.40), kind=kOutput, calls=%fused_computation.clone.1 | convolution fusion | flops 1359249408 | bytes 4718597 | tf_op jit(solution)/shard_map/while/body/eval_jaxpr/kab,kbc->kac/dot_general | solution.py:22
  135.3 0.0 copy-start.1
  135.3 2.5 %fusion.48 = f32[2,384,384]{2,1,0:T(8,128)S(1)} fusion(f32[2,384,384]{2,1,0:T(8,128)S(1)} %get-tuple-element.96, f32[2,384,384]{1,2,0:T(8,128)S(1)} %bitcast.74), kind=kOutput, calls=%fused_computation.49 | convolution fusion | flops 1358954496 | bytes 3538944 | tf_op jit(solution)/shard_map/while/body/eval_jaxpr/kab,kbc->kac/dot_general | solution.py:22
  137.8 0.0 copy-done.1
  137.8 2.5 %fusion.16 = f32[2,384,384]{2,1,0:T(8,128)S(1)} fusion(f32[2,384,384]{2,1,0:T(8,128)S(1)} %fusion.48, f32[2,384,384]{2,1,0:T(8,128)S(1)} %copy-done, f32[2,384,384]{1,2,0:T(8,128)S(1)} %copy-done.1), kind=kOutput, calls=%fused_computation.16 | convolution fusion | flops 1359544320 | bytes 4718592 | tf_op jit(solution)/shard_map/kab,ksbc->ksac/dot_general | solution.py:62
  140.4 2.6 %convolution_bitcast_fusion = f32[2,1,4,2,96,192]{4,5,2,3,0,1:T(8,128)S(1)} fusion(f32[2,384,2,192,1]{1,3,4,2,0:T(8,128)S(1)} %bitcast.77, f32[2,384,4,96,1]{1,3,2,4,0:T(8,128)S(1)} %bitcast.75), kind=kOutput, calls=%fused_computation.11 | convolution fusion | flops 1358954496 | bytes 3538944 | tf_op jit(solution)/shard_map/ksbir,ksbjq->ksijrq/dot_general | solution.py:70
  143.1 0.6 copy.21
  143.7 0.1 copy.22
  143.8 40.3 %all_to_all.25 = f32[2,1,8,96,192]{4,3,0,1,2:T(8,128)S(1)} all-to-all(f32[2,1,8,96,192]{4,3,0,1,2:T(8,128)S(1)} %copy.22), channel_id=1, replica_groups=mesh['drive'=2,'tm'=4,'mom'=2,'col'=2] {'tm','col'}, dimensions={2} | all-to-all | bytes 2359296 | tf_op jit(solution)/shard_map/all_to_all | solution.py:72
  184.1 2.4 %fusion.10 = f32[2,1,8,96,192]{4,2,3,0,1:T(8,128)S(1)} fusion(f32[2,1,8,96,192]{4,3,0,1,2:T(8,128)S(1)} %all_to_all.25), kind=kOutput, calls=%fused_computation.10 | convolution fusion | flops 28312576 | bytes 2359296 | tf_op jit(solution)/shard_map/ft,ktrc->kfrc/dot_general | solution.py:43
  186.5 2.5 %fusion.7 = f32[2,1,8,96,192]{4,2,3,0,1:T(8,128)S(1)} fusion(f32[2,1,8,96,192]{4,3,0,1,2:T(8,128)S(1)} %all_to_all.25), kind=kOutput, calls=%fused_computation.9 | convolution fusion | flops 28312512 | bytes 2359296 | tf_op jit(solution)/shard_map/ft,ktrc->kfrc/dot_general | solution.py:42
  188.9 0.2 pad_maximum_fusion
  189.1 2.6 %copy.24 = f32[2,2,8,96,192]{4,3,2,1,0:T(8,128)} copy(f32[2,2,8,96,192]{4,2,3,0,1:T(8,128)S(1)} %pad_maximum_fusion) | data formatting | bytes 4718592 | tf_op jit(solution)/shard_map/stack | solution.py:44
Async XLA Ops:
  6.5 101.1 %all-gather.2.cloned.1.call-start = ((), (), s32[]{:S(2)}) async-start(), calls=%async_computation.2 | async-start | bytes 10616832 | tf_op jit(solution)/shard_map/all_gather | solution.py:11
  14.0 1.3 copy-start
  135.3 2.5 %copy-start.1 = (f32[2,384,384]{1,2,0:T(8,128)S(1)}, f32[2,384,384]{1,2,0:T(8,128)}, u32[]{:S(2)}) copy-start(f32[2,384,384]{1,2,0:T(8,128)} %copy.20) | copy-start | bytes 3538948
Sparse Core Ops, SparseCore 0:
  14.2 93.4 all-gather.1
where the time goes:
time: 199 us
  waiting for transfers between devices  90.1 us (45%)
  blocking collectives  44.9 us (23%)
  matrix products  38.3 us (19%)
  between operations  13.5 us (7%)
  local copies, waits for them, and re-layouts  10.5 us (5%)
    all_gather x1, waiting for transfers between devices, prefix_2(): pieces = lax.all_gather(value, axis)  90.1 us
    all_to_all x1, blocking collectives, body(): lax.all_to_all(heis, ('tm', 'col'), split_axis=2, concat_axis=1, tiled=True)  40.3 us
    dot_general x8, matrix products, multiply(): jnp.einsum('kab,kbc->kac', left, right, precision=lax.Precision.HIGHEST)  28.2 us
    all_to_all x1, blocking collectives, body(): lax.all_to_all(propagators, 'col', split_axis=1, concat_axis=3, tiled=True)  4.68 us
  transfers between devices with their start and end apart: 1, of which 1 were waited for; matrix products, arithmetic and copies ran while one was open for 1% of the time, Pallas kernels for 0%

commit v1 on v0

v1 whole, which is shorter than its diff:
```python
import functools
import math

import jax
import jax.numpy as jnp
from jax import lax
from jax.experimental import pallas as pl
from jax.experimental.pallas import tpu as pltpu
from jax.sharding import PartitionSpec as P

MESH = pl.DeviceIdType.MESH
NT = (((1,), (1,)), ((), ()))
NN = (((1,), (0,)), ((), ()))


def split(value):
    high = value.astype(jnp.bfloat16)
    low = (value - high.astype(jnp.float32)).astype(jnp.bfloat16)
    return high, low


def dot3(left, right, dims):
    def one(a, b):
        return lax.dot_general(a, b, dims, preferred_element_type=jnp.float32)

    rows = left[0].shape[0]
    both = one(jnp.concatenate(left, axis=0), right[0])
    return both[:rows] + (both[rows:] + one(left[0], right[1]))


def heis_kernel(nz, nc, chunks, u_ref, j_ref, out_ref, jbuf, ubuf, uhi, ulo, whi, wlo, shi, slo, total, pt, down, up, first, got,
                u_send, u_recv, u_local, j_local, i_send, i_recv, c_send, c_recv, x_send, x_recv, h_send, h_recv, f_send, f_recv):
    z = lax.axis_index("tm")
    c = lax.axis_index("col")
    kdev, slices, cw, order = u_ref.shape
    rw = order // nz
    ch = cw // chunks

    barrier = pltpu.get_barrier_semaphore()
    for dz in range(1, nz):
        pl.semaphore_signal(barrier, inc=1, device_id={"tm": lax.rem(z + dz, nz)}, device_id_type=MESH)
    for dc in range(1, nc):
        pl.semaphore_signal(barrier, inc=1, device_id={"col": lax.rem(c + dc, nc)}, device_id_type=MESH)
    own_half = pl.ds(pl.multiple_of(c * cw, 8), cw)
    own_block = pl.ds(pl.multiple_of(z * rw, 8), rw)
    local = []
    for k in range(kdev):
        copy = pltpu.make_async_copy(u_ref.at[k], ubuf.at[k, :, own_half], u_local.at[k])
        copy.start()
        local.append(copy)
    j_copy = pltpu.make_async_copy(j_ref, jbuf, j_local)
    j_copy.start()
    pl.semaphore_wait(barrier, nz + nc - 2)

    def u_copy(k, dc, half):
        return pltpu.make_async_remote_copy(
            u_ref.at[k], ubuf.at[k, :, pl.ds(pl.multiple_of(half * cw, 8), cw)],
            u_send.at[k, dc - 1], u_recv.at[k, dc - 1],
            device_id={"col": lax.rem(c + dc, nc)}, device_id_type=MESH)

    for k in range(kdev):
        for dc in range(1, nc):
            u_copy(k, dc, c).start()

    def part_rows(half, i):
        return pl.ds(pl.multiple_of(half * cw + i * ch, 8), ch)

    def carry_copy(k, i):
        rows = part_rows(c, i)
        return pltpu.make_async_remote_copy(
            pt.at[k, 1, rows], pt.at[k, 0, rows], c_send.at[k, i], c_recv.at[k, i],
            device_id={"tm": lax.rem(z + 1, nz)}, device_id_type=MESH)

    def core_copy(k, i, dc, half):
        rows = part_rows(half, i)
        return pltpu.make_async_remote_copy(
            pt.at[k, pl.ds(0, 2), rows], pt.at[k, pl.ds(0, 2), rows], x_send.at[k, i, dc - 1], x_recv.at[k, i, dc - 1],
            device_id={"col": lax.rem(c + dc, nc)}, device_id_type=MESH)

    def inner_copy(k, dc, half):
        rows = pl.ds(pl.multiple_of(half * cw, 8), cw)
        inner = pl.ds(2, slices - 1)
        return pltpu.make_async_remote_copy(
            pt.at[k, inner, rows], pt.at[k, inner, rows], i_send.at[k, dc - 1], i_recv.at[k, dc - 1],
            device_id={"col": lax.rem(c + dc, nc)}, device_id_type=MESH)

    def block_copy(source, k, peer, mine, slot):
        rows = pl.ds(pl.multiple_of(peer * rw, 8), rw)
        return pltpu.make_async_remote_copy(
            source.at[k, rows], out_ref.at[mine, k], h_send.at[k, slot], h_recv.at[k, slot],
            device_id={"tm": peer}, device_id_type=MESH)

    def first_copy(peer, slot):
        rows = pl.ds(pl.multiple_of(peer * rw, 8), rw)
        return pltpu.make_async_remote_copy(
            first.at[rows], got, f_send.at[slot], f_recv.at[0],
            device_id={"tm": peer}, device_id_type=MESH)

    def send_down(k):
        for d in range(nz - 1, 0, -1):
            @pl.when(z - d >= 0)
            def _():
                block_copy(down, k, lax.rem(z + nz - d, nz), z, d - 1).start()

    def send_up(k):
        for d in range(1, nz):
            @pl.when((z > 0) & (z + d < nz))
            def _():
                block_copy(up, k, lax.rem(z + d, nz), z, nz + d - 1).start()

    for k in range(kdev):
        local[k].wait()
        for dc in range(1, nc):
            u_copy(k, dc, lax.rem(c + nc - dc, nc)).wait_recv()
        product = ubuf[k, 0]
        for s in range(slices):
            uhi[k, s], ulo[k, s] = split(ubuf[k, s])
            if s:
                product = dot3(split(product), (uhi[k, s], ulo[k, s]), NN)
        whi[k], wlo[k] = split(product)

        @pl.when(z == 0)
        def _():
            total[...] = product
            row = lax.broadcasted_iota(jnp.int32, (cw, order), 0) + c * cw
            column = lax.broadcasted_iota(jnp.int32, (cw, order), 1)
            pt[k, 0, own_half] = jnp.where(row == column, 1.0, 0.0).astype(jnp.float32)
            pt[k, 1, own_half] = total[own_half]
            for i in range(chunks):
                carry_copy(k, i).start()

    j_copy.wait()
    for k in range(kdev):
        op = jbuf[k]
        shi[k], slo[k] = split(0.5 * (op + op.T))

    for k in range(kdev):
        for i in range(chunks):
            rows = part_rows(c, i)

            @pl.when(z > 0)
            def _():
                carry_copy(k, i).wait_recv()
                pt[k, 1, rows] = dot3(split(pt[k, 0, rows]), (whi[k], wlo[k]), NN)

            @pl.when((z > 0) & (z < nz - 1))
            def _():
                carry_copy(k, i).start()

            for dc in range(1, nc):
                core_copy(k, i, dc, c).start()
        if slices > 1:
            value = pt[k, 0, own_half]
            for s in range(slices - 1):
                value = dot3(split(value), (uhi[k, s], ulo[k, s]), NN)
                pt[k, 2 + s, own_half] = value
            for dc in range(1, nc):
                inner_copy(k, dc, c).start()
        if k > 0:
            send_up(k - 1)
        lines = jnp.concatenate([pt[k, s, own_half] for s in range(slices + 1)], axis=0)
        weighted = dot3(split(lines), (shi[k], slo[k]), NN)
        for i in range(chunks):
            for dc in range(1, nc):
                core_copy(k, i, dc, lax.rem(c + nc - dc, nc)).wait_recv()
        if slices > 1:
            for dc in range(1, nc):
                inner_copy(k, dc, lax.rem(c + nc - dc, nc)).wait_recv()
        parts = []
        for s in range(slices, -1, -1):
            at = s and (1 if s == slices else s + 1)
            right = split(weighted[at * cw:(at + 1) * cw])
            parts.insert(0, dot3(split(pt[k, at]), right, NT))
            if s == 1:
                down[k] = jnp.concatenate(parts, axis=1)
                send_down(k)
        up[k] = jnp.concatenate(parts[:-1], axis=1)
        for s in range(1, slices):
            at = (k * (slices - 1) + s - 1) * cw
            first[:, at:at + cw] = parts[s]
        out_ref[z, k] = down[k, own_block]

    send_up(kdev - 1)
    for d in range(1, nz):
        @pl.when(z == 0)
        def _():
            first_copy(lax.rem(z + d, nz), d - 1).start()

    for k in range(kdev):
        for d in range(1, nz):
            @pl.when(z + d < nz)
            def _():
                block_copy(down, k, lax.rem(z + d, nz), lax.rem(z + d, nz), d - 1).wait_recv()

            @pl.when(z - d > 0)
            def _():
                block_copy(up, k, lax.rem(z + nz - d, nz), lax.rem(z + nz - d, nz), nz + d - 1).wait_recv()

    @pl.when(z > 0)
    def _():
        first_copy(lax.rem(z, nz), 0).wait_recv()
        for k in range(kdev):
            for s in range(slices):
                if s == 0:
                    block = up[k, own_block][:, :cw]
                else:
                    at = (k * (slices - 1) + s - 1) * cw
                    block = got[:, at:at + cw]
                out_ref[0, k, :, s * cw:(s + 1) * cw] = block

    for k in range(kdev):
        for d in range(1, nz):
            @pl.when(z - d >= 0)
            def _():
                block_copy(down, k, lax.rem(z + nz - d, nz), z, d - 1).wait_send()

            @pl.when((z > 0) & (z + d < nz))
            def _():
                block_copy(up, k, lax.rem(z + d, nz), z, nz + d - 1).wait_send()
        for dc in range(1, nc):
            u_copy(k, dc, c).wait_send()
            if slices > 1:
                inner_copy(k, dc, c).wait_send()
        for i in range(chunks):
            for dc in range(1, nc):
                core_copy(k, i, dc, c).wait_send()

            @pl.when(z < nz - 1)
            def _():
                carry_copy(k, i).wait_send()
    for d in range(1, nz):
        @pl.when(z == 0)
        def _():
            first_copy(lax.rem(z + d, nz), d - 1).wait_send()


def real_dft(values):
    length = len(values)
    if length == 1:
        return [(values[0], None)]
    if length % 2:
        found = []
        for f in range(length):
            re = sum(math.cos(2 * math.pi * f * t / length) * v for t, v in enumerate(values))
            im = sum(-math.sin(2 * math.pi * f * t / length) * v for t, v in enumerate(values))
            found.append((re, im if f else None))
        return found
    half = length // 2
    even, odd = real_dft(values[0::2]), real_dft(values[1::2])
    found = [None] * length
    for f in range(half // 2 + 1):
        (er, ei), (dr, di) = even[f % half], odd[f % half]
        angle = -2 * math.pi * f / length
        if f == 0:
            tr, ti = dr, di
        elif 4 * f == length:
            tr, ti = di, -dr
        else:
            wr, wi = math.cos(angle), math.sin(angle)
            tr = wr * dr if di is None else wr * dr - wi * di
            ti = wi * dr if di is None else wr * di + wi * dr

        def add(a, b, sign):
            if b is None:
                return a
            if a is None:
                return b if sign > 0 else -b
            return a + b if sign > 0 else a - b

        found[f] = (add(er, tr, 1), add(ei, ti, 1))
        found[f + half] = (add(er, tr, -1), add(ei, ti, -1))
    for f in range(length):
        if found[f] is None:
            re, im = found[length - f]
            found[f] = (re, None if im is None else -im)
    return found


def dft_kernel(h_ref, out_ref):
    nz, rows, width = h_ref.shape[0], h_ref.shape[2], h_ref.shape[3]
    length, cw = out_ref.shape[2], out_ref.shape[4]
    scale = 1.0 / math.sqrt(length)
    slices = width // cw
    mine = lax.axis_index("tm") * slices

    def at(slot, s):
        return h_ref[slot, 0, :, s * cw:(s + 1) * cw]

    values = []
    for t in range(nz * slices):
        value = at(t // slices, t % slices)
        if t + 1 < nz * slices:
            value = jnp.where(t < mine, at((t + 1) // slices, (t + 1) % slices), value)
            value = jnp.where(t + 1 == mine, at(0, 0), value)
        values.append(value * scale)
    for f, (re, im) in enumerate(real_dft(values)):
        out_ref[0, 0, f] = re
        out_ref[0, 1, f] = jnp.zeros((rows, cw), jnp.float32) if im is None else im


def body(nz, nc, propagators, current_op):
    turned = jnp.swapaxes(propagators, 2, 3)
    kdev, slices, cw, order = turned.shape
    rw = order // nz
    chunks = 4
    first = max(128, -(-kdev * (slices - 1) * cw // 128) * 128)
    dma = pltpu.SemaphoreType.DMA
    blocks = pl.pallas_call(
        functools.partial(heis_kernel, nz, nc, chunks),
        out_shape=jax.ShapeDtypeStruct((nz, kdev, rw, slices * cw), jnp.float32),
        in_specs=[pl.BlockSpec(memory_space=pl.ANY), pl.BlockSpec(memory_space=pl.ANY)],
        out_specs=pl.BlockSpec(memory_space=pltpu.VMEM),
        scratch_shapes=[
            pltpu.VMEM((kdev, order, order), jnp.float32),
            pltpu.VMEM((kdev, slices, order, order), jnp.float32),
            pltpu.VMEM((kdev, slices, order, order), jnp.bfloat16),
            pltpu.VMEM((kdev, slices, order, order), jnp.bfloat16),
            pltpu.VMEM((kdev, order, order), jnp.bfloat16),
            pltpu.VMEM((kdev, order, order), jnp.bfloat16),
            pltpu.VMEM((kdev, order, order), jnp.bfloat16),
            pltpu.VMEM((kdev, order, order), jnp.bfloat16),
            pltpu.VMEM((order, order), jnp.float32),
            pltpu.VMEM((kdev, slices + 1, order, order), jnp.float32),
            pltpu.VMEM((kdev, order, slices * cw), jnp.float32),
            pltpu.VMEM((kdev, order, slices * cw), jnp.float32),
            pltpu.VMEM((order, first), jnp.float32),
            pltpu.VMEM((rw, first), jnp.float32),
            dma((kdev, nc)), dma((kdev, nc)), dma((kdev,)), dma, dma((kdev, nc)), dma((kdev, nc)),
            dma((kdev, chunks)), dma((kdev, chunks)),
            dma((kdev, chunks, nc)), dma((kdev, chunks, nc)),
            dma((kdev, 2 * nz)), dma((kdev, 2 * nz)), dma((nz,)), dma((1,)),
        ],
        compiler_params=pltpu.CompilerParams(
            collective_id=0, has_side_effects=True, vmem_limit_bytes=60 * 2**20),
    )(turned, current_op)
    length = nz * slices
    step = rw // 2 if rw % 16 == 0 else rw
    return pl.pallas_call(
        dft_kernel,
        grid=(kdev, rw // step),
        out_shape=jax.ShapeDtypeStruct((kdev, 2, length, rw, cw), jnp.float32),
        in_specs=[pl.BlockSpec((nz, 1, step, slices * cw), lambda k, r: (0, k, r, 0))],
        out_specs=pl.BlockSpec((1, 2, length, step, cw), lambda k, r: (k, 0, 0, r, 0)),
        compiler_params=pltpu.CompilerParams(vmem_limit_bytes=32 * 2**20),
    )(blocks)


def solution(mesh):
    return jax.shard_map(
        functools.partial(body, mesh.shape["tm"], mesh.shape["col"]),
        mesh=mesh,
        in_specs=(P(("drive", "mom"), "tm", None, "col"), P("mom", None, None)),
        out_specs=P(("drive", "mom"), None, None, "tm", "col"),
        check_vma=False,
    )
```

time: 199 us -> 60.9 us (0.31)
  the two profiles are of different devices: /device:TPU:0 before, /device:TPU:22 now
where the time goes in v1:
time: 60.9 us; the launch traced here: 60.7 us
  Pallas kernels  59.5 us (98%)
  local copies, waits for them, and re-layouts  1.26 us (2%)
    pallas_call x1, Pallas kernels, body(): pl.pallas_call(functools.partial(heis_kernel, nz, nc, chunks), out_shape=...  56.8 us
    pallas_call x1, Pallas kernels, body(): pl.pallas_call(dft_kernel, grid=(kdev, rw // step), out_shape=jax.ShapeDt...  2.7 us
    unnamed x2, local copies, waits for them, and re-layouts  1.26 us

profile of v1, /device:TPU:22, one launch (start us, length us, event | category | flops | bytes accessed | tf_op | source)
XLA Modules:
  0.0 60.7 jit_solution(15768611712358797286)
XLA Ops:
  0.0 56.8 %shard_map.28.h_ref = f32[4,2,96,384]{3,2,1,0:T(8,128)} custom-call(f32[2,2,192,384]{3,2,1,0:T(8,128)} %bitcast.1, f32[2,384,384]{2,1,0:T(8,128)} %j_ref.1), custom_call_target="tpu_custom_call" | custom-call | tf_op jit(solution)/shard_map/pallas_call | solution.py:308
  56.8 0.0 copy-start
  56.8 1.3 %copy-done = f32[4,2,96,384]{3,2,1,0:T(8,128)S(1)} copy-done((f32[4,2,96,384]{3,2,1,0:T(8,128)S(1)}, f32[4,2,96,384]{3,2,1,0:T(8,128)}, u32[]{:S(2)}) %copy-start) | copy-done | bytes 1179672
  58.0 2.7 %shard_map.29 = f32[2,2,8,96,192]{4,3,2,1,0:T(8,128)} custom-call(f32[4,2,96,384]{3,2,1,0:T(8,128)S(1)} %copy-done), custom_call_target="tpu_custom_call" | custom-call | tf_op jit(solution)/shard_map/pallas_call | solution.py:338
Async XLA Ops:
  56.8 1.3 %copy-start = (f32[4,2,96,384]{3,2,1,0:T(8,128)S(1)}, f32[4,2,96,384]{3,2,1,0:T(8,128)}, u32[]{:S(2)}) copy-start(f32[4,2,96,384]{3,2,1,0:T(8,128)} %shard_map.28.h_ref) | copy-start | bytes 3538948

commit v2 on v1

--- a/solution.py
+++ b/solution.py
@@ -302,7 +302,7 @@
     turned = jnp.swapaxes(propagators, 2, 3)
     kdev, slices, cw, order = turned.shape
     rw = order // nz
-    chunks = 4
+    chunks = 6
     first = max(128, -(-kdev * (slices - 1) * cw // 128) * 128)
     dma = pltpu.SemaphoreType.DMA
     blocks = pl.pallas_call(

time: 60.9 us -> 60.5 us (level)
  no operation moved by 1% of the time
where the time goes in v2:
time: 60.5 us; the launch traced here: 60.4 us
  Pallas kernels  59.1 us (98%)
  local copies, waits for them, and re-layouts  1.26 us (2%)
    pallas_call x1, Pallas kernels, body(): pl.pallas_call(functools.partial(heis_kernel, nz, nc, chunks), out_shape=...  56.4 us
    pallas_call x1, Pallas kernels, body(): pl.pallas_call(dft_kernel, grid=(kdev, rw // step), out_shape=jax.ShapeDt...  2.7 us
    unnamed x2, local copies, waits for them, and re-layouts  1.26 us

profile of v2, /device:TPU:22, one launch (start us, length us, event | category | flops | bytes accessed | tf_op | source)
XLA Modules:
  0.0 60.4 jit_solution(11019352512558166254)
XLA Ops:
  0.0 56.4 %shard_map.28.h_ref = f32[4,2,96,384]{3,2,1,0:T(8,128)} custom-call(f32[2,2,192,384]{3,2,1,0:T(8,128)} %bitcast.1, f32[2,384,384]{2,1,0:T(8,128)} %j_ref.1), custom_call_target="tpu_custom_call" | custom-call | tf_op jit(solution)/shard_map/pallas_call | solution.py:308
  56.4 0.0 copy-start
  56.4 1.3 %copy-done = f32[4,2,96,384]{3,2,1,0:T(8,128)S(1)} copy-done((f32[4,2,96,384]{3,2,1,0:T(8,128)S(1)}, f32[4,2,96,384]{3,2,1,0:T(8,128)}, u32[]{:S(2)}) %copy-start) | copy-done | bytes 1179672
  57.7 2.7 %shard_map.29 = f32[2,2,8,96,192]{4,3,2,1,0:T(8,128)} custom-call(f32[4,2,96,384]{3,2,1,0:T(8,128)S(1)} %copy-done), custom_call_target="tpu_custom_call" | custom-call | tf_op jit(solution)/shard_map/pallas_call | solution.py:338
Async XLA Ops:
  56.4 1.3 %copy-start = (f32[4,2,96,384]{3,2,1,0:T(8,128)S(1)}, f32[4,2,96,384]{3,2,1,0:T(8,128)}, u32[]{:S(2)}) copy-start(f32[4,2,96,384]{3,2,1,0:T(8,128)} %shard_map.28.h_ref) | copy-start | bytes 3538948
